TPU v7x, 128 devices: a whole 4x4x4 slice. The times are simulated.
128 devices in a mesh: dp: 8 (over x, core), blk: 16 (over y, z).
Axes of the slice: x: 4, y: 4, z: 4, core: 2. Of those that a mesh axis runs over, the one named last changes fastest.
Arguments:
- tokens: bfloat16 [8, 2048, 768], P('dp', 'blk'), may hold values from -6 to 6
- lengths: int32 [8], P('dp'), may hold values from 1024 to 2048, as said below
- w_qkv: bfloat16 [768, 2304], P(('dp', 'blk')), may hold values from -0.3125 to 0.3125
- w_out: bfloat16 [768, 768], P(('dp', 'blk')), may hold values from -0.875 to 0.875
- norm_gain: bfloat16 [768], P(('dp', 'blk')), may hold values from 0.5 to 1.5
- norm_shift: bfloat16 [768], P(('dp', 'blk')), may hold values from -3 to 3
- w_up: bfloat16 [768, 3072], P(('dp', 'blk')), may hold values from -0.21875 to 0.21875
- w_down: bfloat16 [3072, 768], P(('dp', 'blk')), may hold values from -0.109375 to 0.109375
- cotangent: bfloat16 [8, 2048, 768], P('dp', 'blk'), may hold values from -6 to 6
Outputs:
- output: bfloat16 [8, 2048, 768], P('dp', 'blk')
- d_tokens: float32 [8, 2048, 768], P('dp', 'blk')
- d_qkv: float32 [768, 2304], P(('dp', 'blk'))
- d_out: float32 [768, 768], P(('dp', 'blk'))
- d_gain: float32 [768], P(('dp', 'blk'))
- d_shift: float32 [768], P(('dp', 'blk'))
- d_up: float32 [768, 3072], P(('dp', 'blk'))
- d_down: float32 [3072, 768], P(('dp', 'blk'))
Inputs may be any that keep to these rules, and one draw needn't show every extreme that they name: `lengths`: each group's value is 2048 (one sequence filling the group) or 2048 // 2 (two sequences of that length, one after the other); both kinds occur in every draw.
All inputs are finite; a program needn't handle non-finite values.
Results may differ from a plain program's by a relative error of at most 0.024.
Values may be sent and summed in bfloat16 or wider, within the bound.
A program may use at most 128 MiB of HBM per device.

v0:
```python
import math

import jax
import jax.numpy as jnp
from jax import lax
from jax.sharding import PartitionSpec as P

HD = 64


big_negative = -1e30


def gelu_tanh(values):
    return jax.nn.gelu(values, approximate=True)


def layer_norm(hidden, gain_vals, shift_vals):
    centred = hidden - jnp.mean(hidden, -1, keepdims=True)
    spread = jnp.mean(centred * centred, -1, keepdims=True)
    return centred * lax.rsqrt(spread + 1e-05) * gain_vals + shift_vals


def unchanged(running):
    return running


def score_parts(queries, query_pos, key_heads, key_pos, doc_len):
    scores = jnp.einsum(
        "gthd,gshd->ghts", queries, key_heads, preferred_element_type=jnp.float32
    ) * HD ** (-0.5)
    causal = key_pos[None, None, :] <= query_pos[None, :, None]
    same_doc = (
        key_pos[None, None, :] // doc_len[:, None, None]
        == query_pos[None, :, None] // doc_len[:, None, None]
    )
    return (scores, (causal & same_doc)[:, None])


def split_piece(piece):
    piece_rows = piece[0].shape[1]
    block_rows = math.gcd(piece_rows, 1024)
    block_count = piece_rows // block_rows
    blocks = tuple(
        (
            jnp.swapaxes(
                member.reshape((member.shape[0], block_count, block_rows) + member.shape[2:]), 0, 1
            )
            for member in piece
        )
    )
    offsets = jnp.arange(block_count, dtype=jnp.int32) * block_rows
    return (blocks, offsets, block_rows)


def as_heads(block, block_rows):
    return block.reshape(block.shape[0], block_rows, -1, HD)


def grad_scores(
    queries,
    grad_heads,
    key_heads,
    value_heads,
    query_pos,
    key_pos,
    doc_len,
    row_top,
    row_total,
    dots,
):
    scores, allowed = score_parts(queries, query_pos, key_heads, key_pos, doc_len)
    probs = (
        jnp.where(allowed, jnp.exp(jnp.abs(scores) - row_top[..., None]), 0.0)
        / row_total[..., None]
    )
    sign_vals = jnp.sign(scores)
    weights = (sign_vals * probs).astype(jnp.bfloat16)
    grad_w = jnp.einsum(
        "gthd,gshd->ghts", grad_heads, value_heads, preferred_element_type=jnp.float32
    )
    grad_s = (sign_vals * probs * (sign_vals * grad_w - dots[..., None])).astype(jnp.bfloat16)
    return (weights, grad_s)


def forward_step(queries, query_pos, doc_len, last_pos, carry, piece):
    blocks, offsets, block_rows = split_piece(piece)

    def forward_inner(running, block_items):
        key_block, value_block, first_row = block_items

        def forward_work(current):
            row_top, row_total, weighted = current
            key_pos = first_row + jnp.arange(block_rows, dtype=jnp.int32)
            scores, allowed = score_parts(
                queries, query_pos, as_heads(key_block, block_rows), key_pos, doc_len
            )
            magnitude = jnp.where(allowed, jnp.abs(scores), big_negative)
            new_top = jnp.maximum(row_top, jnp.max(magnitude, -1))
            expo_vals = jnp.where(allowed, jnp.exp(magnitude - new_top[..., None]), 0.0)
            rescale = jnp.exp(row_top - new_top)
            signed = (jnp.sign(scores) * expo_vals).astype(jnp.bfloat16)
            weighted = weighted * rescale[..., None] + jnp.einsum(
                "ghts,gshd->ghtd",
                signed,
                as_heads(value_block, block_rows),
                preferred_element_type=jnp.float32,
            )
            return (new_top, row_total * rescale + jnp.sum(expo_vals, -1), weighted)

        return (lax.cond(first_row <= last_pos, forward_work, unchanged, running), None)

    carry, _ = lax.scan(forward_inner, carry, blocks + (offsets,))
    return carry


def key_side_step(queries, grad_heads, query_pos, doc_len, last_pos, row_top, row_total, dots):

    def step(carry, piece, start):
        blocks, offsets, block_rows = split_piece(piece)

        def step_inner(running, block_items):
            key_block, value_block, first_row = block_items

            def step_work(current):
                key_pos = first_row + jnp.arange(block_rows, dtype=jnp.int32)
                key_heads = as_heads(key_block, block_rows)
                weights, grad_s = grad_scores(
                    queries,
                    grad_heads,
                    key_heads,
                    as_heads(value_block, block_rows),
                    query_pos,
                    key_pos,
                    doc_len,
                    row_top,
                    row_total,
                    dots,
                )
                grad_q = current[0] + jnp.einsum(
                    "ghts,gshd->gthd", grad_s, key_heads, preferred_element_type=jnp.float32
                )
                buffer = current[1]
                grad_k = jnp.einsum(
                    "ghts,gthd->gshd", grad_s, queries, preferred_element_type=jnp.float32
                ) * HD ** (-0.5)
                grad_v = jnp.einsum(
                    "ghts,gthd->gshd", weights, grad_heads, preferred_element_type=jnp.float32
                )
                group_count = grad_k.shape[0]
                joined = jnp.concatenate(
                    [
                        grad_k.reshape(group_count, block_rows, -1),
                        grad_v.reshape(group_count, block_rows, -1),
                    ],
                    2,
                )
                previous = lax.dynamic_slice_in_dim(buffer, first_row, block_rows, 1)
                buffer = lax.dynamic_update_slice_in_dim(buffer, previous + joined, first_row, 1)
                return (grad_q, buffer)

            return (lax.cond(first_row <= last_pos, step_work, unchanged, running), None)

        carry, _ = lax.scan(step_inner, carry, blocks + (offsets,))
        return carry

    return step


def body(tokens, lengths, w_qkv, w_out, norm_gain, norm_shift, w_up, w_down, cotangent):
    group_count, tok_rows, width = tokens.shape
    heads_count = width // HD
    flat_rows = group_count * tok_rows
    scale_factor = HD ** (-0.5)
    query_pos = lax.axis_index("blk") * tok_rows + jnp.arange(tok_rows, dtype=jnp.int32)
    last_pos = query_pos[tok_rows - 1]
    inputs = tokens.reshape(flat_rows, width)
    qkv_all, out_all = (
        lax.all_gather(w_qkv, ("dp", "blk"), axis=0, tiled=True),
        lax.all_gather(w_out, ("dp", "blk"), axis=0, tiled=True),
    )
    qkv_r = jnp.dot(inputs, qkv_all, preferred_element_type=jnp.float32).astype(jnp.bfloat16)
    qkv_r = qkv_r.reshape(group_count, tok_rows, 3 * width)
    queries = qkv_r[:, :, :width].reshape(group_count, tok_rows, heads_count, HD)
    key_rows = qkv_r[:, :, width : 2 * width]
    value_rows = qkv_r[:, :, 2 * width :]
    start_state = (
        jnp.full((group_count, heads_count, tok_rows), big_negative, jnp.float32),
        jnp.zeros((group_count, heads_count, tok_rows), jnp.float32),
        jnp.zeros((group_count, heads_count, tok_rows, HD), jnp.float32),
    )
    row_top, row_total, weighted = forward_step(
        queries,
        query_pos,
        lengths,
        last_pos,
        start_state,
        (
            lax.all_gather(key_rows, "blk", axis=1, tiled=True),
            lax.all_gather(value_rows, "blk", axis=1, tiled=True),
        ),
    )
    attn_heads = weighted / row_total[..., None]
    attn_tok = jnp.transpose(attn_heads, (0, 2, 1, 3))
    attn_r = attn_tok.reshape(flat_rows, width).astype(jnp.bfloat16)
    hidden = inputs.astype(jnp.float32) + jnp.dot(
        attn_r, out_all, preferred_element_type=jnp.float32
    )
    gain_all, shift_all, up_all, down_all = (
        lax.all_gather(norm_gain, ("dp", "blk"), axis=0, tiled=True),
        lax.all_gather(norm_shift, ("dp", "blk"), axis=0, tiled=True),
        lax.all_gather(w_up, ("dp", "blk"), axis=0, tiled=True),
        lax.all_gather(w_down, ("dp", "blk"), axis=0, tiled=True),
    )
    gain_f = gain_all.astype(jnp.float32)
    shift_f = shift_all.astype(jnp.float32)
    normed_f, norm_pull = jax.vjp(layer_norm, hidden, gain_f, shift_f)
    normed_r = normed_f.astype(jnp.bfloat16)
    pre_act = jnp.dot(normed_r, up_all, preferred_element_type=jnp.float32)
    active_f, gelu_pull = jax.vjp(gelu_tanh, pre_act)
    active_r = active_f.astype(jnp.bfloat16)
    output = (hidden + jnp.dot(active_r, down_all, preferred_element_type=jnp.float32)).astype(
        jnp.bfloat16
    )
    qkv_all, out_all = (
        lax.all_gather(w_qkv, ("dp", "blk"), axis=0, tiled=True),
        lax.all_gather(w_out, ("dp", "blk"), axis=0, tiled=True),
    )
    gain_all, shift_all, up_all, down_all = (
        lax.all_gather(norm_gain, ("dp", "blk"), axis=0, tiled=True),
        lax.all_gather(norm_shift, ("dp", "blk"), axis=0, tiled=True),
        lax.all_gather(w_up, ("dp", "blk"), axis=0, tiled=True),
        lax.all_gather(w_down, ("dp", "blk"), axis=0, tiled=True),
    )
    grad_y = cotangent.reshape(flat_rows, width)
    grad_down = jnp.einsum("tf,td->fd", active_r, grad_y, preferred_element_type=jnp.float32)
    grad_active = jnp.einsum("td,fd->tf", grad_y, down_all, preferred_element_type=jnp.float32)
    grad_pre = gelu_pull(grad_active)[0].astype(jnp.bfloat16)
    grad_up = jnp.einsum("td,tf->df", normed_r, grad_pre, preferred_element_type=jnp.float32)
    grad_normed = jnp.einsum("tf,df->td", grad_pre, up_all, preferred_element_type=jnp.float32)
    grad_ln, grad_gain, grad_shift = norm_pull(grad_normed)
    grad_hidden = grad_y.astype(jnp.float32) + grad_ln
    grad_hidden_r = grad_hidden.astype(jnp.bfloat16)
    grad_out = jnp.einsum("td,te->de", attn_r, grad_hidden_r, preferred_element_type=jnp.float32)
    grad_attn = jnp.einsum("te,de->td", grad_hidden_r, out_all, preferred_element_type=jnp.float32)
    grad_heads = grad_attn.astype(jnp.bfloat16).reshape(group_count, tok_rows, heads_count, HD)
    dots = jnp.transpose(jnp.sum(grad_heads.astype(jnp.float32) * attn_tok, -1), (0, 2, 1))
    zero_heads = jnp.zeros((group_count, tok_rows, heads_count, HD), jnp.float32)
    back_fn = key_side_step(
        queries, grad_heads, query_pos, lengths, last_pos, row_top, row_total, dots
    )
    group_rows = lax.axis_size("blk") * tok_rows
    back_state = (zero_heads, jnp.zeros((group_count, group_rows, 2 * width), jnp.float32))
    back_result = back_fn(
        back_state,
        (
            lax.all_gather(key_rows, "blk", axis=1, tiled=True),
            lax.all_gather(value_rows, "blk", axis=1, tiled=True),
        ),
        jnp.int32(0),
    )
    grad_q = back_result[0]
    grad_kv = lax.psum_scatter(
        back_result[1].astype(jnp.bfloat16), "blk", scatter_dimension=1, tiled=True
    ).astype(jnp.float32)
    grad_qkv = jnp.concatenate(
        [grad_q.reshape(group_count, tok_rows, width) * scale_factor, grad_kv], 2
    )
    grad_qkv = grad_qkv.astype(jnp.bfloat16).reshape(flat_rows, 3 * width)
    grad_qkv_w = jnp.einsum("td,te->de", inputs, grad_qkv, preferred_element_type=jnp.float32)
    grad_inputs = grad_hidden + jnp.einsum(
        "te,de->td", grad_qkv, qkv_all, preferred_element_type=jnp.float32
    )
    owned = (
        lax.psum_scatter(grad_qkv_w, ("dp", "blk"), scatter_dimension=0, tiled=True),
        lax.psum_scatter(grad_out, ("dp", "blk"), scatter_dimension=0, tiled=True),
        lax.psum_scatter(grad_gain, ("dp", "blk"), scatter_dimension=0, tiled=True),
        lax.psum_scatter(grad_shift, ("dp", "blk"), scatter_dimension=0, tiled=True),
        lax.psum_scatter(grad_up, ("dp", "blk"), scatter_dimension=0, tiled=True),
        lax.psum_scatter(grad_down, ("dp", "blk"), scatter_dimension=0, tiled=True),
    )
    return (
        output.reshape(group_count, tok_rows, width),
        grad_inputs.reshape(group_count, tok_rows, width),
        owned[0],
        owned[1],
        owned[2],
        owned[3],
        owned[4],
        owned[5],
    )


def solution(mesh):
    placed = (
        P("dp", "blk", None),
        P("dp"),
        P(("dp", "blk"), None),
        P(("dp", "blk"), None),
        P(("dp", "blk")),
        P(("dp", "blk")),
        P(("dp", "blk"), None),
        P(("dp", "blk"), None),
        P("dp", "blk", None),
    )
    return jax.shard_map(
        body,
        mesh=mesh,
        in_specs=placed,
        out_specs=(
            P("dp", "blk", None),
            P("dp", "blk", None),
            P(("dp", "blk"), None),
            P(("dp", "blk"), None),
            P(("dp", "blk")),
            P(("dp", "blk")),
            P(("dp", "blk"), None),
            P(("dp", "blk"), None),
        ),
        check_vma=False,
    )
```

profile of v0, /device:TPU:2, one launch (start us, length us, event | category | flops | bytes accessed | tf_op | source)
XLA Modules:
  0.0 1388.2 jit_solution(10864939523607900826)
XLA Ops:
  9.4 69.9 %all-gather.16.cloned.1.call-done = bf16[128,6,2304]{2,1,0:T(8,128)(2,1)} async-done(((bf16[1,6,2304]{2,1,0:T(8,128)(2,1)}), bf16[128,6,2304]{2,1,0:T(8,128)(2,1)}) %all-gather.16.cloned.1.call-update) | async-done | bytes 3538960 | tf_op jit(solution)/shard_map/all_gather | solution.py:179
  79.4 6.6 reshape.468
  91.8 63.7 %all-reduce.10 = (bf16[768]{0:T(1024)(128)(2,1)S(1)}, bf16[768]{0:T(1024)(128)(2,1)S(1)}) all-reduce(bf16[768]{0:T(1024)(128)(2,1)S(1)} %dynamic-update-slice.1, bf16[768]{0:T(1024)(128)(2,1)S(1)} %dynamic-update-slice), channel_id=1, replica_groups=mesh['dp'=8,'blk'=16] {'dp','blk'}, use_global_device_ids=true, to_apply=%add.1 | all-reduce | flops 1536 | bytes 6144
  160.6 52.0 %all-gather.20.cloned.1.call-done = bf16[128,6,3072]{2,1,0:T(8,128)(2,1)} async-done(((bf16[1,6,3072]{2,1,0:T(8,128)(2,1)}), bf16[128,6,3072]{2,1,0:T(8,128)(2,1)}) %all-gather.20.cloned.1.call-update) | async-done | bytes 4718608 | tf_op jit(solution)/shard_map/all_gather | solution.py:212
  212.6 7.7 reshape.472
  220.4 41.9 %all-gather.12.cloned.1.call-done = bf16[1,2048,768]{2,1,0:T(8,128)(2,1)} async-done(((bf16[1,128,768]{2,1,0:T(8,128)(2,1)}), bf16[1,2048,768]{2,1,0:T(8,128)(2,1)}) %all-gather.12.cloned.1.call-update) | async-done | bytes 3145744 | tf_op jit(solution)/shard_map/all_gather | solution.py:200
  265.4 46.3 %all-gather.10.cloned.1.call-done = bf16[1,2048,768]{2,1,0:T(8,128)(2,1)} async-done(((bf16[1,128,768]{2,1,0:T(8,128)(2,1)}), bf16[1,2048,768]{2,1,0:T(8,128)(2,1)}) %all-gather.10.cloned.1.call-update) | async-done | bytes 3145744 | tf_op jit(solution)/shard_map/all_gather | solution.py:199
  317.3 33.8 %while.28 = (s32[]{:T(128)}, f32[1,12,128]{2,1,0:T(8,128)S(1)}, f32[1,12,128]{2,1,0:T(8,128)S(1)}, f32[1,12,128,64]{2,3,1,0:T(8,128)}, s32[2]{0:T(128)}, /*index...) while((s32[]{:T(128)}, f32[1,12,128]{2,1,0:T(8,128)S(1)}, ...), condition=%wide.region_5.8_spmd.clone, body=%wide.region_0.7_spmd.clone.sunk | while | flops 431570560 | bytes 29936976 | solution.py:113
  320.4 15.5 %conditional.6 = ((f32[1,12,128]{2,1,0:T(8,128)S(1)}, f32[1,12,128]{2,1,0:T(8,128)S(1)}, f32[1,12,128,64]{2,3,1,0:T(8,128)})) conditional(s32[]{:T(128)} %convert_element_type.133, (f32[1,12,128]{2,1,0:T(8,128)S(1)}, f32[1,12,128]{2,1,0:T(8,128)S(1)}, f32[1,12,128,64]{2,3,1,0:T(8,128)}) %tuple.95, (s32[]{:T(128)}, s32[]{:T(128)}, s32[1]{0:T(128)}, ...), branch_computations={%region_1.1_spmd, %region_2.6_spmd} | conditional | flops 431570560 | bytes 29936200 | solution.py:111
  328.6 5.6 fusion.15
  359.6 19.9 %all-gather.14.cloned.1.call-done = bf16[3072,768]{1,0:T(8,128)(2,1)} async-done(((bf16[24,768]{1,0:T(8,128)(2,1)}), bf16[3072,768]{1,0:T(8,128)(2,1)}) %all-gather.14.cloned.1.call-update) | async-done | bytes 4718608 | tf_op jit(solution)/shard_map/all_gather | solution.py:213
  384.3 5.0 multiply_reduce_fusion
  395.0 6.2 broadcast_in_dim.93
  401.3 66.8 %while.29 = (s32[]{:T(128)}, f32[1,128,12,64]{1,3,2,0:T(8,128)}, f32[1,2048,1536]{1,2,0:T(8,128)}, s32[2]{0:T(128)}, s32[]{:T(128)}, /*index=5*/bf16[2,1,1024,76...) while((s32[]{:T(128)}, f32[1,128,12,64]{1,3,2,0:T(8,128)}, ...), condition=%wide.region_14.17_spmd.clone, body=%wide.region_11.16_spmd.clone.sunk | while | flops 1040952448 | bytes 79111608 | solution.py:164
  404.5 59.9 %conditional.7 = ((f32[1,128,12,64]{1,3,2,0:T(8,128)}, f32[1,2048,1536]{1,2,0:T(8,128)})) conditional(s32[]{:T(128)} %convert_element_type.134, (f32[1,128,12,64]{1,3,2,0:T(8,128)}, f32[1,2048,1536]{1,2,0:T(8,128)}) %tuple.98, (bf16[2,1,1024,768]{2,3,1,0:T(8,128)(2,1)}, s32[]{:T(128)}, bf16[1,128,12,64]{1,3,2,0:T(8,128)(2,1)S(1)}, s32[]{:T(128)}, ...), branch_computations={%region_12.14_spmd, %region_13.15_spmd} | conditional | flops 1040952448 | bytes 79110792 | solution.py:162
  426.8 7.6 maximum_add_fusion
  434.4 30.0 %dynamic_update_slice.4 = f32[1,2048,1536]{1,2,0:T(8,128)} dynamic-update-slice(f32[1,2048,1536]{1,2,0:T(8,128)} %get-tuple-element.309, f32[1,1024,1536]{1,2,0:T(8,128)} %maximum_add_fusion, s32[]{:T(128)} %constant.89.clone, s32[]{:T(128)S(6)} %select_n.32, s32[]{:T(128)} %constant.89.clone) | dynamic-update-slice | bytes 12582916 | tf_op jit(solution)/shard_map/while/body/eval_jaxpr/cond/branch_1_fun/dynamic_update_slice | solution.py:159
  468.0 8.2 convert_element_type.96
  476.3 30.4 %copy.56 = bf16[1,2048,1536]{2,0,1:T(2,128)(2,1)} copy(bf16[1,2048,1536]{1,2,0:T(8,128)(2,1)} %convert_element_type.96) | data formatting | bytes 12582912
  506.6 9.0 copy.62
  516.7 138.1 %reduce-scatter.12.cloned.1.call-done = bf16[128,1536]{1,0:T(8,128)(2,1)} async-done(((bf16[2048,1536]{1,0:T(8,128)(2,1)}), bf16[128,1536]{1,0:T(8,128)(2,1)}) %reduce-scatter.12.cloned.1.call-update) | async-done | bytes 393232
  662.3 5.2 fusion.55
  669.9 5.1 fusion.66
  675.0 327.4 %fusion.68 = (f32[8,768]{1,0:T(8,128)S(1)}, f32[8,3072]{1,0:T(8,128)S(1)}) fusion(f32[768,768]{1,0:T(8,128)S(1)} %fusion.72, f32[768,3072]{1,0:T(8,128)} %fusion.66), kind=kCustom, calls=%all-reduce-scatter.2 | all-reduce-scatter fusion | flops 3932161 | bytes 11919360
  1006.2 34.5 %collective-permute-start.28 = (f32[8,768]{1,0:T(8,128)S(1)}, f32[8,768]{1,0:T(8,128)S(1)}, u32[]{:S(2)}, u32[]{:S(2)}) collective-permute-start(f32[8,768]{1,0:T(8,128)S(1)} %get-tuple-element.570), channel_id=1, source_target_pairs={{0,29},{1,30},{2,31},{3,32},{4,33},{5,34},{6,35},{7,36},{8,37},{9,... | collective-permute-start | bytes 73736
  1040.8 8.6 collective-permute-start.31
  1063.6 8.1 collective-permute-start.21
  1203.1 67.0 %all-reduce.9 = (f32[768]{0:T(1024)S(1)}, f32[768]{0:T(1024)S(1)}) all-reduce(f32[768]{0:T(1024)S(1)} %copy-done.55, f32[768]{0:T(1024)S(1)} %copy-done.56), channel_id=5, replica_groups=mesh['dp'=8,'blk'=16] {'dp','blk'}, use_global_device_ids=true, to_apply=%region_19.22.clone | all-reduce | flops 1536 | bytes 12288
  1271.3 22.7 %concatenate.16 = f32[262,768]{1,0:T(8,128)S(1)} concatenate(f32[6,768]{1,0:T(8,128)S(1)} %collective-permute-done.31, f32[8,768]{1,0:T(8,128)S(1)} %collective-permute-done.30, f32[8,768]{1,0:T(8,128)S(1)} %collective-permute-done.29, f32[8,768]{1,0:T(8,128)S(1)} %collective-permute-done.28, f32[8,768]{1,0:T(8,128)S(1)} %collective-permute-done.27, ...), dimensions={0} | concatenate | bytes 1609728
  1300.3 5.7 collective-permute-start.34
  1311.5 5.5 collective-permute-done.33
  1319.1 53.7 %concatenate.17 = f32[262,3072]{1,0:T(8,128)} concatenate(f32[6,3072]{1,0:T(8,128)S(1)} %collective-permute-done.63, f32[8,3072]{1,0:T(8,128)S(1)} %collective-permute-done.62, f32[8,3072]{1,0:T(8,128)S(1)} %collective-permute-done.61, f32[8,3072]{1,0:T(8,128)S(1)} %collective-permute-done.60, f32[8,3072]{1,0:T(8,128)S(1)} %collective-permute-done.59, ...), dimensions={0} | concatenate | bytes 6438912
  (356 shorter events, 259.6 us)
Async XLA Ops:
  7.2 72.2 %all-gather.16.cloned.1.call-start = ((), (), s32[]{:S(2)}) async-start(), calls=%async_computation.6 | async-start | bytes 4755456 | tf_op jit(solution)/shard_map/all_gather | solution.py:179
  7.9 149.3 %all-gather.18.cloned.1.call-start = ((), (), s32[]{:S(2)}) async-start(), calls=%async_computation.7 | async-start | bytes 1585152 | tf_op jit(solution)/shard_map/all_gather | solution.py:180
  8.6 204.0 %all-gather.20.cloned.1.call-start = ((), (), s32[]{:S(2)}) async-start(), calls=%async_computation.8 | async-start | bytes 6340608 | tf_op jit(solution)/shard_map/all_gather | solution.py:212
  9.4 252.9 %all-gather.12.cloned.1.call-start = ((), (), s32[]{:S(2)}) async-start(), calls=%async_computation.3 | async-start | bytes 3342336 | tf_op jit(solution)/shard_map/all_gather | solution.py:200
  89.5 222.3 %all-gather.10.cloned.1.call-start = ((), (), s32[]{:S(2)}) async-start(), calls=%async_computation.2 | async-start | bytes 3342336 | tf_op jit(solution)/shard_map/all_gather | solution.py:199
  90.1 289.4 %all-gather.14.cloned.1.call-start = ((), (), s32[]{:S(2)}) async-start(), calls=%async_computation.4 | async-start | bytes 4755456 | tf_op jit(solution)/shard_map/all_gather | solution.py:213
  90.6 564.2 %reduce-scatter.12.cloned.1.call-start = ((), (), s32[]{:S(2)}) async-start(), calls=%async_computation.9 | async-start | bytes 6684672
  515.6 862.8 %all-reduce.14.cloned.1.call-start = ((), (), s32[]{:S(2)}) async-start(), calls=%async_computation.10 | async-start | bytes 14155776
  660.9 720.6 %reduce-scatter.10.cloned.1.call-start = ((), (), s32[]{:S(2)}) async-start(), calls=%async_computation.5 | async-start | bytes 9510912 | tf_op jit(solution)/shard_map/reduce_scatter | solution.py:280
  1002.4 53.5 %collective-permute-start.30 = (f32[8,768]{1,0:T(8,128)S(1)}, f32[8,768]{1,0:T(8,128)S(1)}, u32[]{:S(2)}, u32[]{:S(2)}) collective-permute-start(f32[8,768]{1,0:T(8,128)S(1)} %get-tuple-element.570), channel_id=1, source_target_pairs={{0,31},{1,32},{2,33},{3,34},{4,35},{5,36},{6,37},{7,38},{8,39},{9,... | collective-permute-start | bytes 73736
  1004.3 53.5 %collective-permute-start.29 = (f32[8,768]{1,0:T(8,128)S(1)}, f32[8,768]{1,0:T(8,128)S(1)}, u32[]{:S(2)}, u32[]{:S(2)}) collective-permute-start(f32[8,768]{1,0:T(8,128)S(1)} %get-tuple-element.570), channel_id=1, source_target_pairs={{0,30},{1,31},{2,32},{3,33},{4,34},{5,35},{6,36},{7,37},{8,38},{9,... | collective-permute-start | bytes 73736
  1006.2 53.5 %collective-permute-start.28 = (f32[8,768]{1,0:T(8,128)S(1)}, f32[8,768]{1,0:T(8,128)S(1)}, u32[]{:S(2)}, u32[]{:S(2)}) collective-permute-start(f32[8,768]{1,0:T(8,128)S(1)} %get-tuple-element.570), channel_id=1, source_target_pairs={{0,29},{1,30},{2,31},{3,32},{4,33},{5,34},{6,35},{7,36},{8,37},{9,... | collective-permute-start | bytes 73736
  1055.8 15.9 %collective-permute-start.25 = (f32[8,768]{1,0:T(8,128)S(1)}, f32[8,768]{1,0:T(8,128)S(1)}, u32[]{:S(2)}, u32[]{:S(2)}) collective-permute-start(f32[8,768]{1,0:T(8,128)S(1)} %get-tuple-element.570), channel_id=1, source_target_pairs={{0,26},{1,27},{2,28},{3,29},{4,30},{5,31},{6,32},{7,33},{8,34},{9,... | collective-permute-start | bytes 73736
  1057.8 18.4 %collective-permute-start.24 = (f32[8,768]{1,0:T(8,128)S(1)}, f32[8,768]{1,0:T(8,128)S(1)}, u32[]{:S(2)}, u32[]{:S(2)}) collective-permute-start(f32[8,768]{1,0:T(8,128)S(1)} %get-tuple-element.570), channel_id=1, source_target_pairs={{0,25},{1,26},{2,27},{3,28},{4,29},{5,30},{6,31},{7,32},{8,33},{9,... | collective-permute-start | bytes 73736
  1059.7 18.7 %collective-permute-start.23 = (f32[8,768]{1,0:T(8,128)S(1)}, f32[8,768]{1,0:T(8,128)S(1)}, u32[]{:S(2)}, u32[]{:S(2)}) collective-permute-start(f32[8,768]{1,0:T(8,128)S(1)} %get-tuple-element.570), channel_id=1, source_target_pairs={{0,24},{1,25},{2,26},{3,27},{4,28},{5,29},{6,30},{7,31},{8,32},{9,... | collective-permute-start | bytes 73736
  1061.7 20.8 %collective-permute-start.22 = (f32[8,768]{1,0:T(8,128)S(1)}, f32[8,768]{1,0:T(8,128)S(1)}, u32[]{:S(2)}, u32[]{:S(2)}) collective-permute-start(f32[8,768]{1,0:T(8,128)S(1)} %get-tuple-element.570), channel_id=1, source_target_pairs={{0,23},{1,24},{2,25},{3,26},{4,27},{5,28},{6,29},{7,30},{8,31},{9,... | collective-permute-start | bytes 73736
  1063.6 21.1 %collective-permute-start.21 = (f32[8,768]{1,0:T(8,128)S(1)}, f32[8,768]{1,0:T(8,128)S(1)}, u32[]{:S(2)}, u32[]{:S(2)}) collective-permute-start(f32[8,768]{1,0:T(8,128)S(1)} %get-tuple-element.570), channel_id=1, source_target_pairs={{0,22},{1,23},{2,24},{3,25},{4,26},{5,27},{6,28},{7,29},{8,30},{9,... | collective-permute-start | bytes 73736
  1071.7 14.9 %collective-permute-start.20 = (f32[8,768]{1,0:T(8,128)S(1)}, f32[8,768]{1,0:T(8,128)S(1)}, u32[]{:S(2)}, u32[]{:S(2)}) collective-permute-start(f32[8,768]{1,0:T(8,128)S(1)} %get-tuple-element.570), channel_id=1, source_target_pairs={{0,21},{1,22},{2,23},{3,24},{4,25},{5,26},{6,27},{7,28},{8,29},{9,... | collective-permute-start | bytes 73736
  1090.9 13.4 collective-permute-start.13
  1093.0 13.3 collective-permute-start.12
  1100.7 13.6 collective-permute-start.9
  1104.3 42.6 %collective-permute-start.62 = (f32[8,3072]{1,0:T(8,128)S(1)}, f32[8,3072]{1,0:T(8,128)S(1)}, u32[]{:S(2)}, u32[]{:S(2)}) collective-permute-start(f32[8,3072]{1,0:T(8,128)S(1)} %get-tuple-element.571), channel_id=1, source_target_pairs={{0,31},{1,32},{2,33},{3,34},{4,35},{5,36},{6,37},{7,38},{8,39},{9,... | collective-permute-start | bytes 294920
  1114.3 30.7 %collective-permute-start.63 = (f32[6,3072]{1,0:T(8,128)S(1)}, f32[6,3072]{1,0:T(8,128)S(1)}, u32[]{:S(2)}, u32[]{:S(2)}) collective-permute-start(f32[6,3072]{1,0:T(8,128)S(1)} %slice.20), channel_id=1, source_target_pairs={{0,32},{1,33},{2,34},{3,35},{4,36},{5,37},{6,38},{7,39},{8,40},{9,... | collective-permute-start | bytes 221192
  1135.3 13.5 collective-permute-start.61
  1180.7 14.4 %collective-permute-start.42 = (f32[8,3072]{1,0:T(8,128)S(1)}, f32[8,3072]{1,0:T(8,128)S(1)}, u32[]{:S(2)}, u32[]{:S(2)}) collective-permute-start(f32[8,3072]{1,0:T(8,128)S(1)} %get-tuple-element.571), channel_id=1, source_target_pairs={{0,11},{1,12},{2,13},{3,14},{4,15},{5,16},{6,17},{7,18},{8,19},{9,... | collective-permute-start | bytes 294920
  1183.9 110.2 %collective-permute-start.41 = (f32[8,3072]{1,0:T(8,128)S(1)}, f32[8,3072]{1,0:T(8,128)}, u32[]{:S(2)}, u32[]{:S(2)}) collective-permute-start(f32[8,3072]{1,0:T(8,128)S(1)} %get-tuple-element.571), channel_id=1, source_target_pairs={{0,10},{1,11},{2,12},{3,13},{4,14},{5,15},{6,16},{7,17},{8,18},{9,... | collective-permute-start | bytes 294920
  1187.2 109.7 %collective-permute-start.40 = (f32[8,3072]{1,0:T(8,128)S(1)}, f32[8,3072]{1,0:T(8,128)}, u32[]{:S(2)}, u32[]{:S(2)}) collective-permute-start(f32[8,3072]{1,0:T(8,128)S(1)} %get-tuple-element.571), channel_id=1, source_target_pairs={{0,9},{1,10},{2,11},{3,12},{4,13},{5,14},{6,15},{7,16},{8,17},{9,1... | collective-permute-start | bytes 294920
  1189.1 111.1 %collective-permute-start.39 = (f32[8,3072]{1,0:T(8,128)S(1)}, f32[8,3072]{1,0:T(8,128)}, u32[]{:S(2)}, u32[]{:S(2)}) collective-permute-start(f32[8,3072]{1,0:T(8,128)S(1)} %get-tuple-element.571), channel_id=1, source_target_pairs={{0,8},{1,9},{2,10},{3,11},{4,12},{5,13},{6,14},{7,15},{8,16},{9,17... | collective-permute-start | bytes 294920
  1191.7 114.3 %collective-permute-start.38 = (f32[8,3072]{1,0:T(8,128)S(1)}, f32[8,3072]{1,0:T(8,128)}, u32[]{:S(2)}, u32[]{:S(2)}) collective-permute-start(f32[8,3072]{1,0:T(8,128)S(1)} %get-tuple-element.571), channel_id=1, source_target_pairs={{0,7},{1,8},{2,9},{3,10},{4,11},{5,12},{6,13},{7,14},{8,15},{9,16}... | collective-permute-start | bytes 294920
  1195.1 113.8 %collective-permute-start.37 = (f32[8,3072]{1,0:T(8,128)S(1)}, f32[8,3072]{1,0:T(8,128)}, u32[]{:S(2)}, u32[]{:S(2)}) collective-permute-start(f32[8,3072]{1,0:T(8,128)S(1)} %get-tuple-element.571), channel_id=1, source_target_pairs={{0,6},{1,7},{2,8},{3,9},{4,10},{5,11},{6,12},{7,13},{8,14},{9,15},... | collective-permute-start | bytes 294920
  1294.1 17.4 %collective-permute-start.36 = (f32[8,3072]{1,0:T(8,128)S(1)}, f32[8,3072]{1,0:T(8,128)S(1)}, u32[]{:S(2)}, u32[]{:S(2)}) collective-permute-start(f32[8,3072]{1,0:T(8,128)S(1)} %get-tuple-element.571), channel_id=1, source_target_pairs={{0,5},{1,6},{2,7},{3,8},{4,9},{5,10},{6,11},{7,12},{8,13},{9,14},{... | collective-permute-start | bytes 294920
  1296.9 14.5 %collective-permute-start.35 = (f32[8,3072]{1,0:T(8,128)S(1)}, f32[8,3072]{1,0:T(8,128)S(1)}, u32[]{:S(2)}, u32[]{:S(2)}) collective-permute-start(f32[8,3072]{1,0:T(8,128)S(1)} %get-tuple-element.571), channel_id=1, source_target_pairs={{0,4},{1,5},{2,6},{3,7},{4,8},{5,9},{6,10},{7,11},{8,12},{9,13},{1... | collective-permute-start | bytes 294920
  (108 other events, 2573.6 us)
Sparse Core Ops, SparseCore 0:
  11.1 68.2 all-gather.15
  82.1 61.6 all-gather.17
  147.0 65.5 all-gather.19
  215.2 46.9 all-gather.11
  264.9 46.8 all-gather.9
  314.7 64.6 all-gather.13
  515.7 139.0 reduce-scatter.11
  661.0 171.4 all-reduce.13
  838.9 221.9 reduce-scatter.9
where the time goes:
time: 1410 us; the launch traced here: 1390 us
  blocking collectives  458 us (32%)
  waiting for transfers between devices  391 us (28%)
  local copies, waits for them, and re-layouts  207 us (15%)
  starting transfers between devices  199 us (14%)
  matrix products  64.3 us (5%)
  other arithmetic  32 us (2%)
  loops' own time  21.1 us (1%)
  between operations  15.8 us (1%)
    unnamed x3, blocking collectives  458 us
    unnamed x66, starting transfers between devices  199 us
    unnamed x75, waiting for transfers between devices  161 us
    unnamed x155, local copies, waits for them, and re-layouts  156 us
    all_gather x1, waiting for transfers between devices, body(): lax.all_gather(w_qkv, ('dp', 'blk'), axis=0, tiled=True)  69.9 us
    all_gather x1, waiting for transfers between devices, body(): lax.all_gather(w_up, ('dp', 'blk'), axis=0, tiled=True)  52 us
    all_gather x1, waiting for transfers between devices, body(): lax.all_gather(key_rows, 'blk', axis=1, tiled=True)  46.3 us
    all_gather x1, waiting for transfers between devices, body(): lax.all_gather(value_rows, 'blk', axis=1, tiled=True)  41.9 us
  transfers between devices with their start and end apart: 73, of which 16 were waited for; matrix products, arithmetic and copies ran while one was open for 35% of the time, Pallas kernels for 0%

commit v1 on v0

v1 whole, which is shorter than its diff:
```python
import jax
import jax.numpy as jnp
from jax import lax
from jax.experimental import pallas as pl
from jax.experimental.pallas import tpu as pltpu
from jax.sharding import PartitionSpec as P

MESH = pl.DeviceIdType.MESH
F32 = jnp.float32
BF16 = jnp.bfloat16
NEG = -1e30
LOG2E = 1.4426950408889634
SCALE = 0.125
EXP_SCALE = SCALE * LOG2E
ORDERS = (((("x", "y", "z"), ("y", "z", "x"), ("z", "x", "y")),) * 3)
TILE = 256
TILES = 8
CHUNKS = 4
HEADS_HERE = 12


def dot(a, b):
    return lax.dot_general(a, b, (((1,), (0,)), ((), ())), preferred_element_type=F32)


def dot_nt(a, b):
    return lax.dot_general(a, b, (((1,), (1,)), ((), ())), preferred_element_type=F32)


def turned(a):
    return a.astype(F32).T.astype(BF16)


def kernel(
    x_hbm, len_ref, wqkv_hbm, wout_hbm, gain_ref, shift_ref, wup_hbm, wdown_hbm, dy_hbm,
    out_hbm, dtok_hbm, dgs_ref, fin_r, ddown_ref,
    wqkv_ref, wout_ref, wup_ref, wdown_ref, out_ref, dtok_ref, g_ref, r_ref, s1p2, s2p2, dp1, dp0, dpl, p_ref,
    xf, dyf, lenf, ps, pr, uq, pds, pdr, ud, gss, gsr, wos,
    qkvt, aq, kn, vn, otf, lse_ref, top_ref, total_ref, delta_ref, acc_ref, otb, oth, of, nf, act, slope, turn_ref, xt_ref, dpre, pdown, dxr, dnp, dnx, dhf,
    dot_s, ado, dkt, dvt, dqs, dqh, dqf, dtp, dtx, hid_ref, fin_s, fds, fdr,
    ag_s, ag_r, lg_s, lg_r, rs_s, rs_r, rl_s, rl_r, pl_s, pl_r, pr_s, pr_r, ps_s, ps_r, ex_s, ex_r, gs_s, gs_r, aq_s, aq_r, ot_s, ot_r, do_s, do_r, dq_s, dq_r,
    fin_ss, fin_rs, in_s,
):
    dp, blk = lax.axis_index("dp"), lax.axis_index("blk")
    x, c = dp // 2, lax.rem(dp, 2)
    y, z = blk // 4, lax.rem(blk, 4)
    other = 1 - c
    coord = {"x": x, "y": y, "z": z}

    def place(cx, cc, cy, cz):
        return (2 * cx + cc, 4 * cy + cz)

    def yp(cy):
        return lax.rem(cy, 2) * 2 + cy // 2

    loads = [
        pltpu.make_async_copy(src, dst, in_s.at[n])
        for n, (src, dst) in enumerate(
            (
                (wqkv_hbm, wqkv_ref), (wout_hbm, wout_ref), (wup_hbm, wup_ref), (wdown_hbm, wdown_ref),
                (x_hbm, xf.at[c]), (dy_hbm, dyf.at[c]),
            )
        )
    ]
    for load in loads:
        load.start()
    sibling = place(x, other, y, z)
    drain = []

    def remote(src, dst, ssem, rsem, dev):
        return pltpu.make_async_remote_copy(
            src_ref=src, dst_ref=dst, send_sem=ssem, recv_sem=rsem, device_id=dev, device_id_type=MESH
        )

    def send(src, dst, ssem, rsem, dev):
        copy = remote(src, dst, ssem, rsem, dev)
        if drain:
            copy.wait_send()
        else:
            copy.start()

    def landed(dst, rsem):
        if not drain:
            remote(dst, dst, rsem, rsem, sibling).wait_recv()

    def send_or_copy(src, dst, ssem, rsem, dev, mine):
        if not drain:

            @pl.when(mine)
            def _():
                pltpu.make_async_copy(src, dst, rsem).start()

        @pl.when(jnp.logical_not(mine))
        def _():
            send(src, dst, ssem, rsem, dev)

    barrier = pltpu.get_barrier_semaphore()
    for cc in range(2):

        @pl.loop(0, 16)
        def _(b):
            @pl.when(jnp.logical_or(cc != c, b != blk))
            def _():
                pl.semaphore_signal(barrier, inc=1, device_id=(2 * x + cc, b), device_id_type=MESH)

    for d in range(1, 4):
        far_x = lax.rem(x + d, 4)
        for n in range(4):
            spots = [place(far_x, c, lax.rem(y + n, 4), z)]
            if n == 0:
                spots.append(place(far_x, other, y, z))
            else:
                spots.append(place(far_x, c, y, lax.rem(z + n, 4)))
            for spot in spots:
                pl.semaphore_signal(barrier, inc=1, device_id=spot, device_id_type=MESH)

    own_rows = pl.ds(pl.multiple_of(128 * c, 128), 128)
    other_rows = pl.ds(pl.multiple_of(128 * other, 128), 128)

    def exchanges():
        exchange(0, xf.at[c], xf.at[c])
        exchange(1, dyf.at[c], dyf.at[c])
        exchange(2, lenf.at[c], lenf.at[c])
        send_out_half()
        for n in range(3):
            send_grad_normed(n)
        exchange(7, dhf.at[c], dhf.at[c])
        exchange(8, pdown.at[other_rows], dxr)
        exchange(9, dtp.at[other], dtx)

    def send_out_half():
        exchange(3, g_ref.at[0, 0, 3], wos.at[0])
        exchange(10, g_ref.at[0, 1, :, 3], wos.at[1])
        exchange(11, g_ref.at[0, 2, :, :, 3], wos.at[2])

    def exchange(i, src, dst):
        send(src, dst, ex_s.at[i], ex_r.at[i], sibling)

    def exchanged(i, dst):
        landed(dst, ex_r.at[i])

    unit_y = 2 * (y // 2) + c
    slot = lax.rem(y, 2) * 4 + z
    half = lax.rem(z, 2)
    partner = place(x, c, y, z + 1 - 2 * half)

    def send_strips():
        for b in range(2):
            for at in range(8):
                cc, zz = at // 4, at % 4
                mine = (c == cc) & (z == zz) & (y == unit_y)
                dev = place(x, cc, unit_y, zz)
                send_or_copy(
                    ps.at[b, at], pr.at[b, slot], ps_s.at[8 * b + at], ps_r.at[8 * b + slot], dev, mine
                )
        send(pds, pdr, ps_s.at[16], ps_r.at[16], partner)

    def fill_strip(b, at):
        cc, zz = at // 4, at % 4
        if b == 1:
            f0 = 384 * (2 * zz + cc)
            strip = wup_ref[:, f0 : f0 + 384]
        elif zz < 3:
            strip = wqkv_ref[:, 768 * zz + 384 * cc : 768 * zz + 384 * cc + 384]
        else:
            strip = wout_ref[:, 384 * cc : 384 * cc + 384]
        ps[b, at, 0:6, :] = strip.astype(F32)
        ps[b, at, 6:8, :] = jnp.zeros((2, 384), F32)

    def rows_stage(u, stage):
        for n in range(1, 8 if stage else 16):
            d0, d1 = divmod(n, 2 if stage else 4)
            if stage:
                dev = place(lax.rem(x + d0, 4), lax.rem(c + d1, 2), y, z)
            else:
                dev = place(x, c, lax.rem(y + d0, 4), lax.rem(z + d1, 4))
            at = n - 1 + 15 * stage
            send(gss.at[u, stage], gsr.at[u, at], gs_s.at[u, at], gs_r.at[u, at], dev)

    def rows_sum(u, stage):
        total = gss[u, stage]
        for n in range(7 if stage else 15):
            at = n + 15 * stage
            landed(gsr.at[u, at], gs_r.at[u, at])
            total = total + gsr[u, at]
        gss[u, stage + 1] = total

    for load in loads:
        load.wait()
    for b in range(2):
        for at in range(8):
            fill_strip(b, at)
    wd_left = wdown_ref[:, 0:384].astype(F32)
    wd_right = wdown_ref[:, 384:768].astype(F32)
    pds[...] = jnp.where(half == 0, wd_right, wd_left)
    lenf[c] = jnp.full((8, TILE), len_ref[0], jnp.int32).astype(F32)
    lane = lax.broadcasted_iota(jnp.int32, (1, 768), 1)
    first = 6 * (dp * 16 + blk)

    def own_entries(ref):
        entries = ref[...].astype(F32)
        spread = jnp.zeros((1, 768), F32)
        for n in range(6):
            spread = jnp.where(lane == first + n, entries[:, n : n + 1], spread)
        return spread

    def put_rows(u, first_row, second_row):
        for n in range(3):
            lanes = slice(256 * n, 256 * n + 256)
            gss[u, 0, n : n + 1, :] = first_row[:, lanes]
            gss[u, 0, n + 3 : n + 4, :] = second_row[:, lanes]
        gss[u, 0, 6:8, :] = jnp.zeros((2, 256), F32)

    def get_rows(u):
        return [jnp.concatenate([gss[u, 2, n + m : n + m + 1, :] for n in range(3)], axis=1) for m in (0, 3)]

    put_rows(0, own_entries(gain_ref), own_entries(shift_ref))
    ud[pl.ds(pl.multiple_of(24 * half, 8), 24), :] = jnp.where(half == 0, wd_left, wd_right)
    pl.semaphore_wait(barrier, 55)
    send_strips()
    rows_stage(0, 0)
    exchange(0, xf.at[c], xf.at[c])
    exchange(1, dyf.at[c], dyf.at[c])
    exchange(2, lenf.at[c], lenf.at[c])

    def piece(ref, b, k, px, py, pz):
        at = {"x": px, "y": py, "z": pz}
        return ref.at[(b, k) + tuple(at[axis] for axis in reversed(ORDERS[b][k]))]

    def chunk(ref, b, k, p, value, half_of=None):
        index = [b, k]
        for level in (2, 1, 0):
            axis = ORDERS[b][k][level]
            at = value if level == p else coord[axis]
            if level >= p:
                index.append(yp(at) if axis == "y" else at)
            elif half_of is not None and level == 1:
                index.append(pl.ds(2 * half_of, 2))
            else:
                index.append(slice(None))
        return ref.at[tuple(index)]

    def ring(b, k, p):
        axis = ORDERS[b][k][p]
        here = coord[axis]
        right, left, far = (lax.rem(here + d, 4) for d in (1, 3, 2))

        def dev(value):
            at = {**coord, axis: value}
            return place(at["x"], c, at["y"], at["z"])

        return here, right, left, far, dev(right), dev(left)

    def sem_at(b, k, p):
        return ((b * 3 + k) * 3 + p) * 4

    def direct(b, k, p):
        axis = ORDERS[b][k][p]
        here = coord[axis]
        for d in range(1, 4):
            ahead_of = lax.rem(here + d, 4)
            at = {**coord, axis: ahead_of}
            yield d - 1, ahead_of, place(at["x"], c, at["y"], at["z"]), lax.rem(here + 4 - d, 4)

    def gather_small(b, p):
        for k in range(3):
            own = chunk(g_ref, b, k, p, coord[ORDERS[b][k][p]])
            i = sem_at(b, k, p)
            for n, _, dev, _ in direct(b, k, p):
                send(own, own, ag_s.at[i + n], ag_r.at[i + n], dev)

    def gather_small_end(b, p):
        for k in range(3):
            i = sem_at(b, k, p)
            for n, _, _, behind in direct(b, k, p):
                landed(chunk(g_ref, b, k, p, behind), ag_r.at[i + n])

    def plane(k):
        first, second, _ = ORDERS[0][k]
        for n in range(1, 16):
            d0, d1 = divmod(n, 4)
            ahead_of = {**coord, first: lax.rem(coord[first] + d0, 4), second: lax.rem(coord[second] + d1, 4)}
            behind = {
                **coord, first: lax.rem(coord[first] + 4 - d0, 4), second: lax.rem(coord[second] + 4 - d1, 4)
            }
            dev = place(ahead_of["x"], c, ahead_of["y"], ahead_of["z"])
            yield n - 1, ahead_of, dev, behind

    def tile_at(ref, b, k, at):
        return piece(ref, b, k, at["x"], yp(at["y"]), at["z"])

    def gather_plane(b):
        for k in range(3):
            own = tile_at(g_ref, b, k, coord)
            for n, _, dev, _ in plane(k):
                send(own, own, pl_s.at[k, n], pl_r.at[k, n], dev)

    def gather_plane_end(b):
        for k in range(3):
            for n, _, _, behind in plane(k):
                landed(tile_at(g_ref, b, k, behind), pl_r.at[k, n])

    def reduce_plane(b):
        for k in range(3):
            for n, ahead_of, dev, _ in plane(k):
                send(tile_at(r_ref, b, k, ahead_of), dpl.at[k, n], pr_s.at[k, n], pr_r.at[k, n], dev)

    def reduce_plane_end(b):
        for k in range(3):
            total = tile_at(r_ref, b, k, coord)[...].astype(F32)
            for n in range(15):
                landed(dpl.at[k, n], pr_r.at[k, n])
                total = total + dpl[k, n].astype(F32)
            p_ref[b, pl.ds(16 * k, 16), :] = total

    def gather_near(b):
        for k in range(3):
            here, right, left, far, to_right, to_left = ring(b, k, 2)
            i = (b * 3 + k) * 6
            for h in range(2):
                part = chunk(g_ref, b, k, 2, here, h)
                send(part, part, lg_s.at[i + h], lg_r.at[i + h], to_right)
                part = chunk(g_ref, b, k, 2, here, 1 - h)
                send(part, part, lg_s.at[i + 3 - h], lg_r.at[i + 3 - h], to_left)

    def gather_far(b):
        for k in range(3):
            here, right, left, far, to_right, to_left = ring(b, k, 2)
            i = (b * 3 + k) * 6
            part = chunk(g_ref, b, k, 2, left, 0)
            landed(part, lg_r.at[i])
            send(part, part, lg_s.at[i + 4], lg_r.at[i + 4], to_right)
            part = chunk(g_ref, b, k, 2, right, 1)
            landed(part, lg_r.at[i + 3])
            send(part, part, lg_s.at[i + 5], lg_r.at[i + 5], to_left)

    def gather_end(b):
        for k in range(3):
            here, right, left, far, to_right, to_left = ring(b, k, 2)
            i = (b * 3 + k) * 6
            landed(chunk(g_ref, b, k, 2, left, 1), lg_r.at[i + 1])
            landed(chunk(g_ref, b, k, 2, right, 0), lg_r.at[i + 2])
            landed(chunk(g_ref, b, k, 2, far, 0), lg_r.at[i + 4])
            landed(chunk(g_ref, b, k, 2, far, 1), lg_r.at[i + 5])

    def add_to(part, term):
        if not drain:
            part[...] = part[...] + term[...]

    def reduce_far(b):
        for k in range(3):
            here, right, left, far, to_right, to_left = ring(b, k, 2)
            i = (b * 3 + k) * 6
            send(chunk(r_ref, b, k, 2, far, 0), s1p2.at[b, k, 0], rl_s.at[i], rl_r.at[i], to_right)
            send(chunk(r_ref, b, k, 2, far, 1), s1p2.at[b, k, 1], rl_s.at[i + 1], rl_r.at[i + 1], to_left)
        for k in range(3):
            here, right, left, far, to_right, to_left = ring(b, k, 2)
            i = (b * 3 + k) * 6 + 2
            into = s2p2.at[b, k, 0, pl.ds(2, 2)]
            send(chunk(r_ref, b, k, 2, right, 1), into, rl_s.at[i], rl_r.at[i], to_right)
            into = s2p2.at[b, k, 1, pl.ds(0, 2)]
            send(chunk(r_ref, b, k, 2, left, 0), into, rl_s.at[i + 1], rl_r.at[i + 1], to_left)

    def reduce_near(b):
        for k in range(3):
            here, right, left, far, to_right, to_left = ring(b, k, 2)
            i = (b * 3 + k) * 6
            for n, (beside, dev) in enumerate(((right, to_right), (left, to_left))):
                landed(s1p2.at[b, k, n], rl_r.at[i + n])
                part = chunk(r_ref, b, k, 2, beside, n)
                add_to(part, s1p2.at[b, k, n])
                into = s2p2.at[b, k, n, pl.ds(2 * n, 2)]
                send(part, into, rl_s.at[i + 4 + n], rl_r.at[i + 4 + n], dev)

    def reduce_end(b):
        for k in range(3):
            here = coord[ORDERS[b][k][2]]
            i = (b * 3 + k) * 6
            for n in range(2):
                landed(s2p2.at[b, k, n, pl.ds(2 - 2 * n, 2)], rl_r.at[i + 2 + n])
                landed(s2p2.at[b, k, n, pl.ds(2 * n, 2)], rl_r.at[i + 4 + n])
            part = chunk(r_ref, b, k, 2, here)
            total = part[...].astype(F32) + s2p2[b, k, 0].astype(F32) + s2p2[b, k, 1].astype(F32)
            part[...] = total.astype(BF16)

    def reduce_small(b, p):
        into = (dp0, dp1)[p]
        for k in range(3):
            i = sem_at(b, k, p)
            for n, ahead_of, dev, _ in direct(b, k, p):
                send(chunk(r_ref, b, k, p, ahead_of), into.at[b, k, n], rs_s.at[i + n], rs_r.at[i + n], dev)

    def reduce_small_end(b, p):
        into = (dp0, dp1)[p]
        for k in range(3):
            i = sem_at(b, k, p)
            part = chunk(r_ref, b, k, p, coord[ORDERS[b][k][p]])
            total = part[...].astype(F32)
            for n in range(3):
                landed(into.at[b, k, n], rs_r.at[i + n])
                total = total + into[b, k, n].astype(F32)
            if p == 0:
                p_ref[b, pl.ds(16 * k, 16), :] = total
            else:
                part[...] = total.astype(BF16)

    def own_unit(b, rows):
        for k in range(3):
            piece(g_ref, b, k, x, yp(y), z)[...] = rows[16 * k : 16 * k + 16]

    def unit(b):
        for n in range(8):
            landed(pr.at[b, n], ps_r.at[8 * b + n])
            uq[b, 6 * n : 6 * n + 6, :] = pr[b, n, 0:6, :]
        own_unit(b, uq[b].astype(BF16))

    unit(0)
    gather_plane(0)
    landed(pdr, ps_r.at[16])
    ud[pl.ds(pl.multiple_of(24 * (1 - half), 8), 24), :] = pdr[...]
    own_unit(2, ud[...].astype(BF16))
    exchanged(0, xf.at[other])

    unit(1)
    gather_small(1, 0)
    gather_small(2, 0)
    gather_plane_end(0)
    rows_sum(0, 0)
    rows_stage(0, 1)
    gather_near(0)
    x_all = xf[...].reshape(256, 768)
    xt_ref[...] = turned(x_all)
    gather_small_end(1, 0)
    gather_small_end(2, 0)
    gather_far(0)
    gather_small(1, 1)
    gather_small(2, 1)
    gather_end(0)

    units = [(px, py) for px in range(4) for py in range(4)]

    def rows_of(b, j, at):
        return jnp.concatenate([piece(g_ref, b, k, px, py, j)[...] for px, py in at for k in range(3)], axis=0)

    def weight(b, j):
        return rows_of(b, j, units)

    def put(b, j, at, rows):
        for n, (px, py) in enumerate(at):
            for k in range(3):
                start = 48 * n + 16 * k
                piece(r_ref, b, k, px, py, j)[...] = rows[start : start + 16]

    def other_half(at):
        parts = [wos[k, px, py] if k == 1 else wos[k, py, px] for px, py in at for k in range(3)]
        return jnp.concatenate(parts, axis=0)

    x_all = xf[...].reshape(256, 768)

    part = dot(x_all, jnp.concatenate([weight(0, j) for j in range(3)], axis=1)).astype(BF16).astype(F32)
    for j in range(3):
        for g in range(2):
            flat = part[128 * g : 128 * g + 128, 384 * j : 384 * j + 384].T.astype(BF16)
            for h in range(6):
                qkvt[6 * g + h, j] = flat[64 * h : 64 * h + 64]

    turn = 3 * y + 3 + z

    def owner_place(cc, m):
        oy = m // 3
        n = lax.rem(m, 3)
        oz = n + jnp.where(n < 3 - oy, 0, 1)
        return place(x, cc, oy, oz), (y == oy) & (z == oz) & (c == cc)

    def send_heads():
        for n in range(HEADS_HERE):
            m = lax.rem(turn + n, HEADS_HERE)
            dev, mine = owner_place(c, m)
            send_or_copy(qkvt.at[m], aq.at[blk], aq_s.at[m], aq_r.at[blk], dev, mine)

    send_heads()
    send_out_half()
    gather_small_end(1, 1)
    gather_near(1)
    gather_small_end(2, 1)
    gather_near(2)

    owner = z != 3 - y
    group = y // 2
    head_slot = 3 * y + z - jnp.where(z > 3 - y, 1, 0)
    exchanged(2, lenf.at[other])

    def blocks_of(ref, first_block, count, j=None):
        at = [first_block + n for n in range(count)]
        return jnp.concatenate([ref[n] if j is None else ref[n, j] for n in at], axis=1)

    def split_bias(ii, kt):
        short = lenf[group, 0:1, :] < 1536.0
        apart = jnp.logical_and(ii >= CHUNKS // 2, kt < CHUNKS // 2)
        return jnp.where(jnp.logical_and(short, apart), NEG, 0.0)

    def sign_of(scores):
        return jnp.clip(scores * 3e38, -1.0, 1.0)

    key_at = lax.broadcasted_iota(jnp.int32, (TILE, TILE), 0)
    query_at = lax.broadcasted_iota(jnp.int32, (TILE, TILE), 1)

    def heads_home(b):
        hy, hz = b // 4, lax.rem(b, 4)
        for cc in range(2):
            mine = (c == cc) & (y == hy) & (z == hz)
            dev = place(x, cc, hy, hz)
            send_or_copy(otb.at[b], oth.at[c, head_slot], ot_s.at[cc, b], ot_r.at[c, head_slot], dev, mine)

    def grads_home(b):
        hy, hz = b // 4, lax.rem(b, 4)
        mine = (y == hy) & (z == hz)
        send_or_copy(
            dqs.at[b], dqh.at[head_slot], dq_s.at[b], dq_r.at[head_slot], place(x, c, hy, hz), mine
        )

    def allowed(size):
        return jnp.where(key_at <= query_at, size, NEG)

    def forward_step(ii, kt, on_diagonal):
        queries = blocks_of(aq, 4 * ii, 4, 0)
        scores = [dot(kn[2 * kt], queries)]
        if on_diagonal:
            later = dot(kn[2 * kt + 1], queries[:, TILE:])
            scores = [[scores[0][:, 0:TILE]], [scores[0][:, TILE:], later]]
            bias = 0.0
        else:
            scores.append(dot(kn[2 * kt + 1], queries))
            scores = [[s[:, TILE * h : TILE * h + TILE] for s in scores] for h in range(2)]
            bias = split_bias(ii, kt)
        for h in range(2):
            size = [jnp.abs(s) * EXP_SCALE for s in scores[h]]
            if on_diagonal:
                size[h] = allowed(size[h])
            most = jnp.max(size[0], axis=0, keepdims=True)
            for more in size[1:]:
                most = jnp.maximum(most, jnp.max(more, axis=0, keepdims=True))
            if on_diagonal:
                top = most
                total = jnp.zeros((1, TILE), F32)
                acc = jnp.zeros((64, TILE), F32)
            else:
                top = jnp.maximum(top_ref[h], most + bias)
                rescale = jnp.exp2(top_ref[h] - top)
                total = total_ref[h] * rescale
                acc = acc_ref[h] * rescale
            for n in range(len(size)):
                expo = jnp.exp2(size[n] - (top - bias))
                total = total + jnp.sum(expo, axis=0, keepdims=True)
                weights = (expo * sign_of(scores[h][n])).astype(BF16)
                acc = acc + dot(blocks_of(aq, 4 * kt + 2 * n, 2, 2), weights)
            top_ref[h] = top
            total_ref[h] = total
            acc_ref[h] = acc

    def forward_first(ii):
        for b in range(4):
            landed(aq.at[4 * ii + b], aq_r.at[4 * ii + b])
        for n in range(2):
            kn[2 * ii + n] = turned(blocks_of(aq, 4 * ii + 2 * n, 2, 1))
            vn[2 * ii + n] = turned(blocks_of(aq, 4 * ii + 2 * n, 2, 2))
        forward_step(ii, ii, True)

    def forward_last(ii):
        for h in range(2):
            heads = acc_ref[h] / total_ref[h]
            otf[2 * ii + h] = heads
            lse_ref[2 * ii + h] = top_ref[h] + jnp.log(total_ref[h]) * LOG2E
            heads = heads.astype(BF16)
            for b in range(2):
                otb[4 * ii + 2 * h + b] = heads[:, 128 * b : 128 * b + 128]
        for n in range(4):
            heads_home(4 * ii + lax.rem(z + n, 4))

    def run_steps(first, step, last, at_first, at_step):
        @pl.loop(0, CHUNKS)
        def _(n):
            ii = n if first is forward_first else CHUNKS - 1 - n

            @pl.when(owner)
            def _():
                first(ii)

            for at, work in at_first.items():
                pl.when(n == at)(lambda work=work: (work(), None)[1])

            @pl.loop(0, ii)
            def _(t):
                @pl.when(owner)
                def _():
                    step(ii, ii - 1 - t, False)

                for (at, at_t), work in at_step.items():
                    pl.when((n == at) & (t == at_t))(lambda work=work: (work(), None)[1])

            @pl.when(owner)
            def _():
                last(ii)

    run_steps(
        forward_first,
        forward_step,
        forward_last,
        {},
        {},
    )
    gather_far(1)
    gather_far(2)

    def from_heads(ref, g):
        return jnp.concatenate([ref[6 * g + h] for h in range(6)], axis=0).astype(F32).T.astype(BF16)

    for h in range(2):
        for m in range(HEADS_HERE):
            landed(oth.at[h, m], ot_r.at[h, m])
        for g in range(2):
            of[h, 128 * g : 128 * g + 128, :] = from_heads(oth.at[h], g)
    for n, k in ((3, 0), (10, 1), (11, 2)):
        exchanged(n, wos.at[k])
    rows_sum(0, 1)
    gain, shift = get_rows(0)

    def normal(hidden):
        centred = hidden - jnp.mean(hidden, axis=1, keepdims=True)
        inv = lax.rsqrt(jnp.mean(centred * centred, axis=1, keepdims=True) + 1e-05)
        return centred * inv, inv

    attn = jnp.concatenate([of[0], of[1]], axis=1)
    by_both = dot(attn, jnp.concatenate([weight(0, 3), other_half(units)], axis=1))
    by_own, by_other = by_both[:, 0:384], by_both[:, 384:768]
    mixed = jnp.concatenate(
        [jnp.where(c == 0, by_own, by_other), jnp.where(c == 0, by_other, by_own)], axis=1
    )
    hid_ref[...] = x_all.astype(F32) + mixed
    nf[...] = (normal(hid_ref[...])[0] * gain + shift).astype(BF16)
    exchanged(1, dyf.at[other])
    gather_end(1)

    n_all = nf[...]
    dy_all = dyf[...].reshape(256, 768)

    def down(hh, j):
        at = [(yy, zp, k) for yy in (0, 2, 1, 3) for zp in range(2) for k in range(3)]
        return jnp.concatenate([piece(g_ref, 2, k, j, yy, 2 * zp + hh)[...] for yy, zp, k in at], axis=0)

    def up_pair(n):
        return jnp.concatenate([weight(1, 2 * n), weight(1, 2 * n + 1)], axis=1)

    def down_pair(n):
        return jnp.concatenate(
            [jnp.concatenate([down(0, 2 * n + m), down(1, 2 * n + m)], axis=1) for m in range(2)], axis=0
        )

    root = 0.7978845608028654

    @pl.loop(0, 2)
    def _(j):
        pre = dot(n_all, up_pair(j))
        squared = pre * pre
        bent = jnp.tanh(root * pre * (1.0 + 0.044715 * squared))
        act[j] = (0.5 * pre * (1.0 + bent)).astype(BF16)
        slope[j] = 0.5 * (1.0 + bent) + 0.5 * pre * (1.0 - bent * bent) * (root * (1.0 + 0.134145 * squared))

    @pl.loop(0, 2)
    def _(j):
        grad = dot(turned(act[j]), dy_all).astype(BF16)
        for m in range(2):
            for hh in range(2):
                for n, yy in enumerate((0, 2, 1, 3)):
                    for zp in range(2):
                        for k in range(3):
                            at = 384 * m + 96 * n + 48 * zp + 16 * k
                            tile = grad[at : at + 16, 384 * hh : 384 * hh + 384]
                            piece(r_ref, 2, k, 2 * j + m, yy, 2 * zp + hh)[...] = tile

    reduce_far(2)
    gather_end(2)

    @pl.loop(0, 2)
    def _(j):
        dpre[j] = (dot_nt(dy_all, down_pair(j)) * slope[j]).astype(BF16)

    def some_rows(j, n):
        at = [divmod(t, 3) for t in range(16 * n, 16 * n + 16)]
        return jnp.concatenate([piece(g_ref, 1, k, *units[u], j)[...] for u, k in at], axis=0)

    def send_grad_normed(n):
        exchange((6, 4, 5)[n], dnp.at[n, other_rows], dnx.at[n])

    for n in range(3):
        part = [
            dot_nt(dpre[j], jnp.concatenate([some_rows(2 * j, n), some_rows(2 * j + 1, n)], axis=1))
            for j in range(2)
        ]
        dnp[n] = part[0] + part[1]
        send_grad_normed(n)

    xhat, inv = normal(hid_ref[own_rows, :])
    for n in range(3):
        exchanged((6, 4, 5)[n], dnx.at[n])
    grad_normed = jnp.concatenate([dnp[n, own_rows, :] + dnx[n] for n in range(3)], axis=1)
    put_rows(
        1,
        jnp.sum(grad_normed * xhat, axis=0, keepdims=True),
        jnp.sum(grad_normed, axis=0, keepdims=True),
    )
    grad_hat = grad_normed * gain
    grad_ln = inv * (
        grad_hat
        - jnp.mean(grad_hat, axis=1, keepdims=True)
        - xhat * jnp.mean(grad_hat * xhat, axis=1, keepdims=True)
    )
    grad_hidden = dyf[c].astype(F32) + grad_ln
    dtok_ref[...] = grad_hidden
    dhf[c] = grad_hidden.astype(BF16)
    exchange(7, dhf.at[c], dhf.at[c])
    own_columns = pl.ds(pl.multiple_of(384 * c, 128), 384)
    other_columns = pl.ds(pl.multiple_of(384 * other, 128), 384)
    dh_sides = jnp.concatenate([dhf[c, :, own_columns], dhf[c, :, other_columns]], axis=1)
    flat = dot(jnp.concatenate([weight(0, 3), other_half(units)], axis=1), turned(dh_sides)).astype(BF16)
    for h in range(12):
        dot_s[h] = flat[64 * h : 64 * h + 64]

    def send_head_grads():
        for n in range(12):
            h = lax.rem(turn + n, 12)
            dev, mine = owner_place(h // 6, 6 * c + lax.rem(h, 6))
            send_or_copy(dot_s.at[h], ado.at[blk], do_s.at[h], do_r.at[blk], dev, mine)

    send_head_grads()
    rows_stage(1, 0)
    turn_ref[...] = turned(n_all)

    @pl.loop(0, 2)
    def _(j):
        grad = dot(turn_ref[...], dpre[j]).astype(BF16)
        put(1, 2 * j, units, grad[:, 0:384])
        put(1, 2 * j + 1, units, grad[:, 384:768])

    exchanged(7, dhf.at[other])
    dh_own = dhf[:, :, own_columns].reshape(256, 384)
    reduce_near(2)
    reduce_far(1)

    @pl.loop(0, 2)
    def _(hh):
        grad = dot(turned(of[hh]), dh_own).astype(BF16)
        put(0, 3, [(2 * hh + n, py) for n in range(2) for py in range(4)], grad)


    @pl.when(owner)
    def _():
        dkt[...] = jnp.zeros_like(dkt)
        dvt[...] = jnp.zeros_like(dvt)

    def backward_step(ii, kt, on_diagonal):
        queries = blocks_of(aq, 4 * ii, 4, 0)
        grads = blocks_of(ado, 4 * ii, 4)
        bias = 0.0 if on_diagonal else split_bias(ii, kt)
        grad_s = [[], []]
        for n in range(2):
            tile = 2 * kt + n
            h0 = n if on_diagonal else 0
            lanes = slice(TILE * h0, 2 * TILE)
            scores = dot(kn[tile], queries[:, lanes])
            grad_w = dot(vn[tile], grads[:, lanes])
            all_weights = []
            for h in range(h0, 2):
                at = slice(TILE * (h - h0), TILE * (h - h0) + TILE)
                signs = sign_of(scores[:, at])
                probs = jnp.exp2(jnp.abs(scores[:, at]) * EXP_SCALE - (lse_ref[2 * ii + h] - bias))
                if on_diagonal and h == n:
                    probs = jnp.where(key_at <= query_at, probs, 0.0)
                weights = probs * signs
                all_weights.append(weights.astype(BF16))
                grad_s[n].append((weights * (signs * grad_w[:, at] - delta_ref[h])).astype(BF16))
            dkt[tile] += dot_nt(queries[:, lanes], jnp.concatenate(grad_s[n], axis=1))
            dvt[tile] += dot_nt(grads[:, lanes], jnp.concatenate(all_weights, axis=1))
        for h in range(2):
            terms = [g[h - len(g)] if on_diagonal else g[h] for g in grad_s if len(g) + h >= 2]
            keys = blocks_of(aq, 4 * kt, 2 * len(terms), 1)
            term = dot(keys, jnp.concatenate(terms, axis=0))
            if on_diagonal:
                acc_ref[h] = term
            else:
                acc_ref[h] += term

    def backward_first(ii):
        for b in range(4):
            landed(ado.at[4 * ii + b], do_r.at[4 * ii + b])
        for h in range(2):
            grads = blocks_of(ado, 4 * ii + 2 * h, 2).astype(F32)
            delta_ref[h] = jnp.sum(grads * otf[2 * ii + h], axis=0, keepdims=True)
        backward_step(ii, ii, True)

    def backward_last(ii):
        for h in range(2):
            grad_q = (acc_ref[h] * SCALE).astype(BF16)
            grad_k = (dkt[2 * ii + h] * SCALE).astype(BF16)
            grad_v = dvt[2 * ii + h].astype(BF16)
            for b in range(2):
                at = 4 * ii + 2 * h + b
                lanes = slice(128 * b, 128 * b + 128)
                dqs[at, 0] = grad_q[:, lanes]
                dqs[at, 1] = grad_k[:, lanes]
                dqs[at, 2] = grad_v[:, lanes]
        for n in range(4):
            grads_home(4 * ii + lax.rem(z + n, 4))

    def emit_output():
        exchanged(8, dxr)
        out_ref[...] = (hid_ref[own_rows, :] + pdown[own_rows, :] + dxr[...]).astype(BF16)
        pltpu.make_async_copy(out_ref, out_hbm, in_s.at[0]).start()

    run_steps(
        backward_first,
        backward_step,
        backward_last,
        {},
        {(0, 2): lambda: reduce_near(1)},
    )

    to_core = lax.rem(y, 2)

    def send_sums(b):
        for s in range(8):
            if not drain:
                fin_s[b, s, 0:6, :] = p_ref[b, 6 * s : 6 * s + 6, :]
                fin_s[b, s, 6:8, :] = jnp.zeros((2, 384), F32)
            to_y = 2 * (y // 2) + s // 4
            mine = (c == to_core) & (y == to_y) & (z == s % 4)
            dev, at = place(x, to_core, to_y, s % 4), c * 4 + z
            send_or_copy(
                fin_s.at[b, s], fin_r.at[b, at], fin_ss.at[9 * b + s], fin_rs.at[9 * b + at], dev, mine
            )
        if b == 1:
            if not drain:
                fds[...] = p_ref[2, pl.ds(pl.multiple_of(24 * (1 - half), 8), 24), :]
            send(fds, fdr, fin_ss.at[8], fin_rs.at[8], partner)

    for m in range(HEADS_HERE):
        landed(dqh.at[m], dq_r.at[m])
    @pl.loop(0, 3)
    def _(j):
        halves_of = [jnp.concatenate([dqh[6 * g + h, j] for h in range(6)], axis=0) for g in range(2)]
        dqf[j] = jnp.concatenate(halves_of, axis=1)
        put(0, j, units, dot_nt(xt_ref[...], dqf[j]).astype(BF16))

    reduce_far(0)
    reduce_end(2)
    reduce_small(2, 1)
    reduce_end(1)
    reduce_small(1, 1)
    rows_sum(1, 0)
    rows_stage(1, 1)

    @pl.loop(0, 3)
    def _(j):
        term = dot(weight(0, j), dqf[j])
        for g in range(2):
            lanes = slice(128 * g, 128 * g + 128)
            dtp[g] = jnp.where(j == 0, term[:, lanes], dtp[g] + term[:, lanes])

    exchange(9, dtp.at[other], dtx)
    reduce_near(0)
    reduce_small_end(2, 1)
    reduce_small(2, 0)
    reduce_small_end(1, 1)
    reduce_small(1, 0)

    pdown[...] = dot(act[0], down_pair(0))
    pdown[...] += dot(act[1], down_pair(1))
    exchange(8, pdown.at[other_rows], dxr)
    rows_sum(1, 1)
    reduce_small_end(2, 0)
    reduce_small_end(1, 0)
    send_sums(1)
    reduce_end(0)
    reduce_plane(0)
    exchanged(9, dtx)
    dtok_ref[...] = dtok_ref[...] + (dtp[c] + dtx[...]).T
    pltpu.make_async_copy(dtok_ref, dtok_hbm, in_s.at[1]).start()
    drain.append(True)
    exchanges()
    send_strips()
    send_heads()
    send_head_grads()
    for b in range(3):
        gather_near(b)
        gather_far(b)
        reduce_far(b)
        reduce_near(b)
        for p in range(2):
            if b > 0:
                gather_small(b, p)
                reduce_small(b, p)
    gather_plane(0)
    for u in range(2):
        for stage in range(2):
            rows_stage(u, stage)

    @pl.when(owner)
    def _():
        @pl.loop(0, 16)
        def _(b):
            heads_home(b)
            grads_home(b)

    drain.clear()
    emit_output()
    reduce_plane_end(0)

    send_sums(0)
    kept = p_ref[2, pl.ds(pl.multiple_of(24 * half, 8), 24), :]
    gather_row = lax.broadcasted_iota(jnp.int32, (768, 128), 0)
    gather_lane = lax.broadcasted_iota(jnp.int32, (768, 128), 1)
    pick = jnp.where((gather_row == first + gather_lane) & (gather_lane < 6), 1.0, 0.0)
    sums_of_rows = jnp.concatenate(get_rows(1) + [jnp.zeros((6, 768), F32)], axis=0)
    dgs_ref[...] = lax.dot_general(
        sums_of_rows, pick, (((1,), (0,)), ((), ())), precision=lax.Precision.HIGHEST, preferred_element_type=F32
    )
    landed(fdr, fin_rs.at[8])
    ddown_ref[:, 0:384] = jnp.where(half == 0, kept, fdr[...])
    ddown_ref[:, 384:768] = jnp.where(half == 0, fdr[...], kept)
    for b in range(2):
        for at in range(8):
            landed(fin_r.at[b, at], fin_rs.at[9 * b + at])

    pltpu.make_async_copy(out_ref, out_hbm, in_s.at[0]).wait()
    pltpu.make_async_copy(dtok_ref, dtok_hbm, in_s.at[1]).wait()
    drain.append(True)
    reduce_plane(0)
    send_sums(0)
    send_sums(1)


def write_results(out_ref, dtok_ref, dgs_ref, fin_ref, ddown_ref, *results):
    output, d_tokens, d_qkv, d_out, d_gain, d_shift, d_up, d_down = results
    output[...] = out_ref[...]
    d_tokens[...] = dtok_ref[...]
    d_gain[...] = dgs_ref[0:1, 0:6]
    d_shift[...] = dgs_ref[1:2, 0:6]
    d_down[...] = ddown_ref[...]
    for at in range(8):
        cc, zz = at // 4, at % 4
        if zz < 3:
            d_qkv[:, 768 * zz + 384 * cc : 768 * zz + 384 * cc + 384] = fin_ref[0, at, 0:6, :]
        else:
            d_out[:, 384 * cc : 384 * cc + 384] = fin_ref[0, at, 0:6, :]
        f0 = 384 * (2 * zz + cc)
        d_up[:, f0 : f0 + 384] = fin_ref[1, at, 0:6, :]


def layer(tokens, lengths, w_qkv, w_out, norm_gain, norm_shift, w_up, w_down, cotangent):
    rows, width = tokens.shape[1], tokens.shape[2]
    vmem = pl.BlockSpec(memory_space=pltpu.VMEM)
    hbm = pl.BlockSpec(memory_space=pl.ANY)
    dma = pltpu.SemaphoreType.DMA
    scratch = [
        (w_qkv.shape, BF16),
        (w_out.shape, BF16),
        (w_up.shape, BF16),
        (w_down.shape, BF16),
        ((rows, width), BF16),
        ((rows, width), F32),
        ((3, 3, 4, 4, 4, 16, 384), BF16),
        ((3, 3, 4, 4, 4, 16, 384), BF16),
        ((3, 3, 2, 2, 4, 16, 384), BF16),
        ((3, 3, 2, 4, 4, 16, 384), BF16),
        ((3, 3, 3, 4, 16, 384), BF16),
        ((3, 3, 3, 16, 384), BF16),
        ((3, 15, 16, 384), BF16),
        ((3, 48, 384), F32),
        ((2, 128, 768), BF16),
        ((2, 128, 768), BF16),
        ((2, 8, TILE), F32),
        ((2, 8, 8, 384), F32),
        ((2, 8, 8, 384), F32),
        ((2, 48, 384), F32),
        ((24, 384), F32),
        ((24, 384), F32),
        ((48, 384), F32),
        ((2, 3, 8, 256), F32),
        ((2, 22, 8, 256), F32),
        ((3, 4, 4, 16, 384), BF16),
        ((HEADS_HERE, 3, 64, 128), BF16),
        ((16, 3, 64, 128), BF16),
        ((TILES, TILE, 64), BF16),
        ((TILES, TILE, 64), BF16),
        ((TILES, 64, TILE), F32),
        ((TILES, 1, TILE), F32),
        ((2, 1, TILE), F32),
        ((2, 1, TILE), F32),
        ((2, 1, TILE), F32),
        ((2, 64, TILE), F32),
        ((16, 64, 128), BF16),
        ((2, HEADS_HERE, 64, 128), BF16),
        ((2, 256, 384), BF16),
        ((256, 768), BF16),
        ((2, 256, 768), BF16),
        ((2, 256, 768), F32),
        ((768, 256), BF16),
        ((768, 256), BF16),
        ((2, 256, 768), BF16),
        ((256, 768), F32),
        ((128, 768), F32),
        ((3, 256, 256), F32),
        ((3, 128, 256), F32),
        ((2, 128, 768), BF16),
        ((HEADS_HERE, 64, 128), BF16),
        ((16, 64, 128), BF16),
        ((TILES, 64, TILE), F32),
        ((TILES, 64, TILE), F32),
        ((16, 3, 64, 128), BF16),
        ((HEADS_HERE, 3, 64, 128), BF16),
        ((3, 384, 256), BF16),
        ((2, 768, 128), F32),
        ((768, 128), F32),
        ((256, 768), F32),
        ((2, 8, 8, 384), F32),
        ((24, 384), F32),
        ((24, 384), F32),
    ]
    sems = [
        (108,), (108,), (54,), (54,), (108,), (108,), (54,), (54,), (3, 15), (3, 15), (3, 15), (3, 15), (17,), (17,), (12,), (12,), (2, 22), (2, 22),
        (12,), (16,), (2, 16), (2, 12), (12,), (16,), (16,), (12,), (17,), (17,), (6,),
    ]
    results = pl.pallas_call(
        kernel,
        out_shape=(
            jax.ShapeDtypeStruct((rows, width), BF16),
            jax.ShapeDtypeStruct((rows, width), F32),
            jax.ShapeDtypeStruct((8, 128), F32),
            jax.ShapeDtypeStruct((2, 8, 8, 384), F32),
            jax.ShapeDtypeStruct(w_down.shape, F32),
        ),
        in_specs=[hbm, pl.BlockSpec(memory_space=pltpu.SMEM), hbm, hbm, vmem, vmem, hbm, hbm, hbm],
        out_specs=[hbm, hbm, vmem, vmem, vmem],
        scratch_shapes=[pltpu.VMEM(s, t) for s, t in scratch] + [dma(s) for s in sems],
        compiler_params=pltpu.CompilerParams(
            collective_id=0, has_side_effects=True, vmem_limit_bytes=56 * 1024 * 1024
        ),
    )(
        tokens.reshape(rows, width), lengths, w_qkv, w_out, norm_gain.reshape(1, 6), norm_shift.reshape(1, 6),
        w_up, w_down, cotangent.reshape(rows, width),
    )
    output, d_tokens, d_qkv, d_out, d_gain, d_shift, d_up, d_down = pl.pallas_call(
        write_results,
        out_shape=(
            jax.ShapeDtypeStruct((rows, width), BF16),
            jax.ShapeDtypeStruct((rows, width), F32),
            jax.ShapeDtypeStruct(w_qkv.shape, F32),
            jax.ShapeDtypeStruct(w_out.shape, F32),
            jax.ShapeDtypeStruct((1, 6), F32),
            jax.ShapeDtypeStruct((1, 6), F32),
            jax.ShapeDtypeStruct(w_up.shape, F32),
            jax.ShapeDtypeStruct(w_down.shape, F32),
        ),
        in_specs=[vmem] * 5,
        out_specs=[vmem] * 8,
    )(*results)
    return (
        output.reshape(1, rows, width),
        d_tokens.reshape(1, rows, width),
        d_qkv,
        d_out,
        d_gain.reshape(6),
        d_shift.reshape(6),
        d_up,
        d_down,
    )


def solution(mesh):
    by_token = P("dp", "blk", None)
    by_row = P(("dp", "blk"), None)
    by_entry = P(("dp", "blk"))
    return jax.shard_map(
        layer,
        mesh=mesh,
        in_specs=(by_token, P("dp"), by_row, by_row, by_entry, by_entry, by_row, by_row, by_token),
        out_specs=(by_token, by_token, by_row, by_row, by_entry, by_entry, by_row, by_row),
        check_vma=False,
    )
```

time: 1410 us -> 139 us (0.10); the launches traced: 1390 us -> 138 us
  blocking collectives: 458 us -> 0 us
  waiting for transfers between devices: 391 us -> 0 us
  local copies, waits for them, and re-layouts: 207 us -> 0 us
  starting transfers between devices: 199 us -> 0 us
  Pallas kernels: 0 us -> 137 us
  matrix products: 64.3 us -> 0 us
  other arithmetic: 32 us -> 0 us
  loops' own time: 21.1 us -> 0 us
  between operations: 15.8 us -> 1.29 us
    unnamed x3 -> x0, blocking collectives: 458 us -> none
    all_gather x6 -> x0, waiting for transfers between devices: 230 us -> none  [the longest x1 69.9 us: body(): lax.all_gather(w_qkv, ('dp', 'blk'), axis=0, tiled=True)]
    unnamed x66 -> x0, starting transfers between devices: 199 us -> none
    unnamed x75 -> x0, waiting for transfers between devices: 161 us -> none
    unnamed x155 -> x0, local copies, waits for them, and re-layouts: 156 us -> none
    pallas_call x0 -> x2, Pallas kernels: none -> 137 us  [the longest x1 135 us: layer(): pl.pallas_call(kernel, out_shape=(jax.ShapeDtypeStruct((rows, width), BF1...]
    dot_general x19 -> x0, matrix products: 64.3 us -> none  [the longest x1 5.6 us: forward_work(): jnp.einsum('ghts,gshd->ghtd', signed, as_heads(value_block, block_rows),...]
    dynamic_update_slice x1 -> x0, local copies, waits for them, and re-layouts: 30 us -> none  [step_work(): lax.dynamic_update_slice_in_dim(buffer, previous + joined, first_row, 1)]
  transfers between devices with their start and end apart: 73 -> 0, of which waited for: 16 -> 0; matrix products, arithmetic and copies ran while one was open for 35% -> 0% of each run, Pallas kernels for 0% -> 0%
where the time goes in v1:
time: 139 us; the launch traced here: 138 us
  Pallas kernels  137 us (99%)
    pallas_call x1, Pallas kernels, layer(): pl.pallas_call(kernel, out_shape=(jax.ShapeDtypeStruct((rows, width), BF1...  135 us

profile of v1, /device:TPU:2, one launch (start us, length us, event | category | flops | bytes accessed | tf_op | source)
XLA Modules:
  0.0 138.2 jit_solution(15268608898733977949)
XLA Ops:
  1.3 134.8 %shard_map.152 = (bf16[128,768]{1,0:T(8,128)(2,1)}, f32[128,768]{1,0:T(8,128)}, f32[8,128]{1,0:T(8,128)}, f32[2,8,8,384]{3,2,1,0:T(8,128)}, f32[24,768]{1,0:T(8,128)}) custom-call(bf16[128,768]{1,0:T(8,128)(2,1)} %bitcast.8, s32[1]{0:T(128)S(6)} %copy.17.len_ref, bf16[6,2304]{1,0:T(8,128)(2,1)} %wqkv_hbm.1, bf16[6,768]{1,0:T(8,128)(2,1)} %wout_hbm.1, ...), custom_call_target="tpu_custom_call" | custom-call | tf_op jit(solution)/shard_map/pallas_call | solution.py:1033
  136.1 2.1 %shard_map.153 = (bf16[128,768]{1,0:T(8,128)(2,1)}, f32[128,768]{1,0:T(8,128)}, f32[6,2304]{1,0:T(8,128)}, f32[6,768]{1,0:T(8,128)}, f32[1,6]{1,0:T(1,128)}, /*i...) custom-call(bf16[128,768]{1,0:T(8,128)(2,1)} %get-tuple-element.21.out_ref, ...), custom_call_target="tpu_custom_call" | custom-call | tf_op jit(solution)/shard_map/pallas_call | solution.py:1052
